TPU v7x, 32 devices: a whole 2x2x4 slice. The times are simulated.
32 devices in a mesh: dp: 4 (over x, core), expert: 8 (over z, y).
Axes of the slice: x: 2, y: 2, z: 4, core: 2. Of those that a mesh axis runs over, the one named last changes fastest.
Arguments:
- tokens: bfloat16 [128, 7168], P(('dp', 'expert')), may hold values from -6 to 6
- routes: int32 [128, 8], P(('dp', 'expert')), may hold values from 0 to 31, all different within a row; in each aligned block of 4 rows (0 to 3, 4 to 7, ...) at most 2 rows name the same one
- gate_scores: float32 [128, 8], P(('dp', 'expert')), may hold values from 0.1 to 1
- w_gate: bfloat16 [32, 7168, 2048], P('expert', None, 'dp'), may hold values from -0.0625 to 0.0625
- w_up: bfloat16 [32, 7168, 2048], P('expert', None, 'dp'), may hold values from -0.0625 to 0.0625
- w_down: bfloat16 [32, 2048, 7168], P('expert', None, 'dp'), may hold values from -0.125 to 0.125
Outputs:
- combined: bfloat16 [128, 7168], P(('dp', 'expert'))
Inputs may be any that keep to these rules, and one draw needn't show every extreme that they name: `routes`: each row names 8 different experts; among the rows of one device no expert is named more than 2 times, a bound that some block reaches.
All inputs are finite; a program needn't handle non-finite values.
Results may differ from a plain program's by a relative error of at most 0.0057.
Values may be sent and summed in bfloat16 or wider, within the bound.
A program may use at most 192 MiB of HBM per device.

v0:
```python
import jax
import jax.numpy as jnp
from jax import lax
from jax.sharding import PartitionSpec as P

D = 7168
TOPK = 8
E = 32
CAP = 2


def slot_codes(route_block):
    route_list = route_block.reshape(-1)
    onehot = (route_list[:, None] == jnp.arange(E, dtype=jnp.int32)[None, :]).astype(jnp.int32)
    before = jnp.cumsum(onehot, axis=0) - onehot
    return (route_list * CAP + jnp.sum(before * onehot, axis=1)).reshape(route_block.shape)


def selection(route_block):
    codes = slot_codes(route_block)
    hits = codes[None, :, :] == jnp.arange(E * CAP, dtype=jnp.int32)[:, None, None]
    return jnp.any(hits, axis=2).astype(jnp.bfloat16)


def expert_hidden(rows_in, gate_local, up_local):
    gate_part = jnp.einsum("erk,ekf->erf", rows_in, gate_local, preferred_element_type=jnp.float32)
    up_part = jnp.einsum("erk,ekf->erf", rows_in, up_local, preferred_element_type=jnp.float32)
    return (jax.nn.silu(gate_part) * up_part).astype(jnp.bfloat16)


def body(tokens, routes, gate_scores, w_gate, w_up, w_down):
    n_data = lax.axis_size("dp")
    n_group = lax.axis_size("expert")
    local_experts = w_gate.shape[0]
    tok_count = tokens.shape[0]
    all_tokens, all_routes = (
        lax.all_gather(tokens, "dp", axis=0, tiled=True),
        lax.all_gather(routes, "dp", axis=0, tiled=True),
    )
    route_blocks = all_routes.reshape(n_data, tok_count, TOPK)
    chosen = jax.vmap(selection)(route_blocks).reshape(n_data, E, CAP, tok_count)
    token_blocks = all_tokens.reshape(n_data, tok_count, D)
    outgoing = jnp.einsum(
        "decn,dnk->edck", chosen, token_blocks, preferred_element_type=jnp.float32
    ).astype(jnp.bfloat16)
    arrived = lax.all_to_all(outgoing, "expert", split_axis=0, concat_axis=2, tiled=True)
    items = arrived.shape[1]
    merged = arrived.reshape(local_experts, items * arrived.shape[2], D)
    result = expert_hidden(merged, w_gate, w_up)
    hidden_split = result.reshape(local_experts, items, arrived.shape[2], w_gate.shape[2])
    hidden = hidden_split.reshape(local_experts, n_data * n_group * CAP, w_gate.shape[2])
    width_local = w_down.shape[2]
    expert_out = jnp.einsum(
        "erf,efk->erk",
        lax.all_gather(hidden, "dp", axis=2, tiled=True),
        w_down,
        preferred_element_type=jnp.float32,
    ).astype(jnp.bfloat16)
    expert_out = expert_out.reshape(local_experts, n_data, n_group, CAP, width_local)
    returned = lax.all_to_all(
        lax.all_to_all(expert_out, "dp", split_axis=1, concat_axis=4, tiled=True),
        "expert",
        split_axis=2,
        concat_axis=0,
        tiled=True,
    )
    returned = returned.reshape(E * CAP, D)
    codes = slot_codes(routes)
    matches = codes[:, :, None] == jnp.arange(E * CAP, dtype=jnp.int32)[None, None, :]
    weighting = jnp.sum(jnp.where(matches, gate_scores[:, :, None], 0.0), axis=1)
    combined = jnp.dot(weighting, returned.astype(jnp.float32), precision=lax.Precision.HIGHEST)
    return combined.astype(jnp.bfloat16)


def solution(mesh):
    placed = (
        P(("dp", "expert"), None),
        P(("dp", "expert"), None),
        P(("dp", "expert"), None),
        P("expert", None, "dp"),
        P("expert", None, "dp"),
        P("expert", None, "dp"),
    )
    return jax.shard_map(
        body, mesh=mesh, in_specs=placed, out_specs=P(("dp", "expert"), None), check_vma=False
    )
```

profile of v0, /device:TPU:0, one launch (start us, length us, event | category | flops | bytes accessed | tf_op | source)
XLA Modules:
  0.0 237.9 jit_solution(15998013190049495341)
XLA Ops:
  6.5 6.3 %all-gather = s32[4,4,8]{2,1,0:T(4,128)S(1)} all-gather(s32[1,4,8]{2,1,0:T(4,128)} %bitcast.38), channel_id=1, replica_groups=mesh['dp'=4,'expert'=8] {'dp'}, dimensions={0}, use_global_device_ids=true | all-gather | bytes 640 | tf_op jit(solution)/shard_map/all_gather | solution.py:38
  12.8 0.1 eq.63
  12.9 0.1 fusion.4
  13.0 0.1 reduce_window_sum.23
  13.0 0.2 select_reduce_fusion
  13.3 0.1 reduce_sum.35
  13.4 0.1 fusion.5
  13.5 0.1 copy.18
  13.6 6.3 %all-gather.1 = bf16[4,4,7168]{2,1,0:T(4,128)(2,1)S(1)} all-gather(bf16[1,4,7168]{2,1,0:T(4,128)(2,1)} %bitcast.37), channel_id=1, replica_groups=mesh['dp'=4,'expert'=8] {'dp'}, dimensions={0}, use_global_device_ids=true | all-gather | bytes 286720 | tf_op jit(solution)/shard_map/all_gather | solution.py:37
  19.9 1.1 fusion
  21.0 3.8 %copy.20 = bf16[32,4,2,7168]{3,2,1,0:T(2,128)(2,1)S(1)} copy(bf16[32,4,2,7168]{3,0,2,1:T(8,128)(2,1)S(1)} %fusion) | data formatting | bytes 7340032 | tf_op jit(solution)/shard_map/convert_element_type | solution.py:45
  24.8 88.2 %all_to_all.48 = bf16[32,4,2,7168]{3,2,1,0:T(2,128)(2,1)S(1)} all-to-all(bf16[32,4,2,7168]{3,2,1,0:T(2,128)(2,1)S(1)} %copy.20), channel_id=1, replica_groups=mesh['dp'=4,'expert'=8] {'expert'}, dimensions={0} | all-to-all | bytes 7340032 | tf_op jit(solution)/shard_map/all_to_all | solution.py:46
  112.9 5.5 %copy.31 = bf16[8,4,4,2,7168]{4,3,0,2,1:T(2,128)(2,1)} copy(bf16[8,4,4,2,7168]{4,3,2,1,0:T(2,128)(2,1)S(1)} %bitcast.32) | data formatting | bytes 7340032 | tf_op jit(solution)/shard_map/all_to_all | solution.py:46
  118.4 8.4 %reshape.42 = bf16[4,64,7168]{2,1,0:T(8,128)(2,1)} reshape(bf16[4,4,8,2,7168]{4,3,2,1,0:T(2,128)(2,1)} %bitcast.33) | data formatting | bytes 7340032 | tf_op jit(solution)/shard_map/reshape | solution.py:48
  126.8 13.1 %fusion.7 = f32[4,64,512]{2,1,0:T(8,128)S(1)} fusion(bf16[4,64,7168]{2,1,0:T(8,128)(2,1)} %reshape.42, bf16[4,7168,512]{2,1,0:T(8,128)(2,1)} %param.9), kind=kOutput, calls=%fused_computation.21 | convolution fusion | flops 1879048192 | bytes 33554432 | tf_op jit(solution)/shard_map/erk,ekf->erf/dot_general | solution.py:26
  139.9 12.9 %fusion.1 = bf16[4,64,512]{2,1,0:T(8,128)(2,1)} fusion(bf16[4,64,7168]{2,1,0:T(8,128)(2,1)S(1)} %copy-done, bf16[4,7168,512]{2,1,0:T(8,128)(2,1)} %param.10, f32[4,64,512]{2,1,0:T(8,128)S(1)} %fusion.7), kind=kOutput, calls=%fused_computation.6 | convolution fusion | flops 1879834624 | bytes 33816576 | tf_op jit(solution)/shard_map/erk,ekf->erf/dot_general | solution.py:27
  152.8 15.9 %all-gather.4.cloned.1.call-done = bf16[4,64,2048]{2,1,0:T(8,128)(2,1)} async-done(((bf16[4,64,512]{2,1,0:T(8,128)(2,1)}), bf16[4,64,2048]{2,1,0:T(8,128)(2,1)}) %all-gather.4.cloned.1.call-update) | async-done | bytes 1048592 | tf_op jit(solution)/shard_map/all_gather | solution.py:55
  168.8 14.6 %convolution_convert_fusion.2 = bf16[4,64,1792]{2,1,0:T(8,128)(2,1)S(1)} fusion(bf16[4,64,2048]{2,1,0:T(8,128)(2,1)} %all-gather.4.cloned.1.call-done, bf16[4,2048,1792]{2,1,0:T(8,128)(2,1)} %param.11), kind=kOutput, calls=%fused_computation.4 | convolution fusion | flops 1879506944 | bytes 31326208 | tf_op jit(solution)/shard_map/erf,efk->erk/dot_general | solution.py:53
  183.4 0.3 reshape.43
  183.8 0.1 copy.22
  183.9 15.5 %all_to_all.49 = bf16[4,4,8,2,1792]{4,2,3,0,1:T(8,128)(2,1)S(1)} all-to-all(bf16[4,4,8,2,1792]{4,2,3,0,1:T(8,128)(2,1)S(1)} %copy.22), channel_id=1, replica_groups=mesh['dp'=4,'expert'=8] {'dp'}, dimensions={1} | all-to-all | bytes 1835008 | tf_op jit(solution)/shard_map/all_to_all | solution.py:61
  199.3 0.7 copy.26
  200.1 1.3 reshape.55
  201.3 5.5 %all-to-all-start.2 = ((bf16[4,1,8,2,7168]{4,3,0,1,2:T(2,128)(2,1)}), bf16[4,1,8,2,7168]{4,3,0,1,2:T(2,128)(2,1)S(1)}, u32[]{:S(2)}, u32[]{:S(2)}) async-start(bf16[4,1,8,2,7168]{4,3,0,1,2:T(2,128)(2,1)} %reshape.55), calls=%async_computation.2 | async-start | bytes 1835008 | tf_op jit(solution)/shard_map/all_to_all | solution.py:60
  206.8 0.1 eq.56
  206.9 0.1 fusion.6
  207.1 0.2 select_reduce_fusion.2
  207.2 0.1 reduce_sum.32
  207.3 0.1 select_reduce_fusion.1
  207.4 22.2 %all-to-all-done.2 = bf16[4,1,8,2,7168]{4,3,0,1,2:T(2,128)(2,1)S(1)} async-done(((bf16[4,1,8,2,7168]{4,3,0,1,2:T(2,128)(2,1)}), bf16[4,1,8,2,7168]{4,3,0,1,2:T(2,128)(2,1)S(1)}, u32[]{:S(2)}, u32[]{:S(2)}) %all-to-all-start.2) | async-done | bytes 917536 | tf_op jit(solution)/shard_map/all_to_all | solution.py:60
  229.7 0.3 reshape.44
  230.0 1.1 convolution_convert_fusion.1
  (11 shorter events, 0.1 us)
Async XLA Ops:
  6.5 162.2 %all-gather.4.cloned.1.call-start = ((), (), s32[]{:S(2)}) async-start(), calls=%async_computation.3 | async-start | bytes 1310720 | tf_op jit(solution)/shard_map/all_gather | solution.py:55
  126.8 13.1 %copy-start = (bf16[4,64,7168]{2,1,0:T(8,128)(2,1)S(1)}, bf16[4,64,7168]{2,1,0:T(8,128)(2,1)}, u32[]{:S(2)}) copy-start(bf16[4,64,7168]{2,1,0:T(8,128)(2,1)} %reshape.42) | copy-start | bytes 11010052
  183.4 23.5 %copy-start.1 = (s32[4,8]{1,0:T(4,128)S(1)}, s32[4,8]{1,0:T(4,128)}, u32[]{:S(2)}) copy-start(s32[4,8]{1,0:T(4,128)} %param.7) | copy-start | bytes 388
  183.4 23.9 %copy-start.2 = (f32[4,8]{1,0:T(4,128)S(1)}, f32[4,8]{1,0:T(4,128)}, u32[]{:S(2)}) copy-start(f32[4,8]{1,0:T(4,128)} %param.8) | copy-start | bytes 388
  201.3 28.3 %all-to-all-start.2 = ((bf16[4,1,8,2,7168]{4,3,0,1,2:T(2,128)(2,1)}), bf16[4,1,8,2,7168]{4,3,0,1,2:T(2,128)(2,1)S(1)}, u32[]{:S(2)}, u32[]{:S(2)}) async-start(bf16[4,1,8,2,7168]{4,3,0,1,2:T(2,128)(2,1)} %reshape.55), calls=%async_computation.2 | async-start | bytes 1835008 | tf_op jit(solution)/shard_map/all_to_all | solution.py:60
Sparse Core Ops, SparseCore 0:
  152.9 15.7 all-gather.3
where the time goes:
time: 238 us
  blocking collectives  116 us (49%)
  matrix products  42.8 us (18%)
  waiting for transfers between devices  38.2 us (16%)
  local copies, waits for them, and re-layouts  20.9 us (9%)
  between operations  13.5 us (6%)
  starting transfers between devices  5.52 us (2%)
    all_to_all x1, blocking collectives, body(): lax.all_to_all(outgoing, 'expert', split_axis=0, concat_axis=2, tiled=True)  88.2 us
    all_to_all x1, waiting for transfers between devices, body(): lax.all_to_all(lax.all_to_all(expert_out, 'dp', split_axis=1, concat_axis...  22.2 us
    all_gather x1, waiting for transfers between devices, body(): lax.all_gather(hidden, 'dp', axis=2, tiled=True)  15.9 us
    all_to_all x1, blocking collectives, body(): lax.all_to_all(expert_out, 'dp', split_axis=1, concat_axis=4, tiled=True)  15.5 us
    dot_general x1, matrix products, body(): jnp.einsum('erf,efk->erk', lax.all_gather(hidden, 'dp', axis=2, tiled=Tru...  14.6 us
    dot_general x1, matrix products, expert_hidden(): jnp.einsum('erk,ekf->erf', rows_in, gate_local, preferred_element_type=jn...  13.1 us
    dot_general x1, matrix products, expert_hidden(): jnp.einsum('erk,ekf->erf', rows_in, up_local, preferred_element_type=jnp....  12.9 us
    reshape x1, local copies, waits for them, and re-layouts, body(): merged = arrived.reshape(local_experts, items * arrived.shape[2], D)  8.4 us
  transfers between devices with their start and end apart: 2, of which 2 were waited for; matrix products, arithmetic and copies ran while one was open for 0% of the time, Pallas kernels for 0%

commit v1 on v0

v1 whole, which is shorter than its diff:
```python
import functools

import jax
import jax.numpy as jnp
from jax import lax
from jax.experimental import pallas as pl
from jax.experimental.pallas import tpu as pltpu
from jax.sharding import PartitionSpec as P

MESH = pl.DeviceIdType.MESH
F32, BF16 = jnp.float32, jnp.bfloat16
PARTS = 4
CHUNKS = 7
LANES = 128

ORDERS = (("a", "b", "x", "c"), ("x", "b", "a", "c"))


def kernel(
    sizes, ring, down_ring,
    tokens, routes, scores, w_gate, w_up, w_down, out,
    g0, g1, rows, score, weights, acc, hidden, down, total, sent, arrived, fin, fin_in,
    tok_send, tok_recv, w_sem, d_sem, h_send, h_recv, r_send, r_recv, f_send, f_recv,
):
    n = dict(zip("abxc", sizes))
    n_dp, n_e = n["x"] * n["c"], n["a"] * n["b"]
    tok, width = tokens.shape
    local, _, ff = w_gate.shape
    slab = width // PARTS
    half = slab // 2
    group = n_dp * tok
    count = n_e * group
    chunk = w_down.shape[2] // CHUNKS
    steps = local * PARTS

    dp, ex = lax.axis_index("dp"), lax.axis_index("expert")
    me = dict(a=ex // n["b"], b=lax.rem(ex, n["b"]), x=dp // n["c"], c=lax.rem(dp, n["c"]))

    def device(at):
        return (at["x"] * n["c"] + at["c"], at["a"] * n["b"] + at["b"])

    def w_copies(i):
        e, q, slot = i // PARTS, lax.rem(i, PARTS), lax.rem(i, ring)
        part = pl.ds(pl.multiple_of(q * slab, slab), slab)
        return [
            pltpu.make_async_copy(w.at[e, part, :], weights.at[slot, j], w_sem.at[slot, j])
            for j, w in enumerate((w_gate, w_up))
        ]

    def d_copy(i):
        slot = lax.rem(i, down_ring)
        columns = pl.ds(pl.multiple_of(i * chunk, chunk), chunk)
        return pltpu.make_async_copy(w_down.at[:, :, columns], down.at[slot], d_sem.at[slot])

    @pl.loop(0, ring)
    def _(i):
        for copy in w_copies(i):
            copy.start()

    barrier = pltpu.get_barrier_semaphore()
    for k in range(1, n_dp):
        pl.semaphore_signal(barrier, inc=1, device_id=(lax.rem(dp + k, n_dp), ex), device_id_type=MESH)

    @pl.loop(1, n_e)
    def _(k):
        pl.semaphore_signal(barrier, inc=1, device_id=(dp, lax.rem(ex + k, n_e)), device_id_type=MESH)

    t32 = tokens[...].astype(F32)
    lanes = lax.broadcasted_iota(jnp.int32, (tok, LANES), 1)
    dense = jnp.zeros((tok, LANES), F32)
    for k in range(routes.shape[1]):
        dense += jnp.where(lanes == routes[:, k : k + 1], scores[:, k : k + 1], 0.0)
    terms, rest = [], dense
    for _ in range(3):
        term = rest.astype(BF16).astype(F32)
        terms.append(term)
        rest = rest - term
    terms.append(jnp.zeros((tok, LANES), F32))
    own = (me["a"], me["b"], me["x"], me["c"])
    cut = [t32[:, q * slab : (q + 1) * slab] for q in range(PARTS)]
    g0[own + (slice(None), slice(0, half))] = jnp.concatenate([p[:, :half] for p in cut], 0).astype(BF16)
    g0[own + (slice(None), slice(half, half + LANES))] = jnp.concatenate(terms, 0).astype(BF16)
    g1[own] = jnp.concatenate([p[:, half:] for p in cut], 0).astype(BF16)

    pl.semaphore_wait(barrier, n_dp - 1 + n_e - 1)

    def gather_copies(stream, stage):
        order, buf = ORDERS[stream], (g0, g1)[stream]
        axis = order[stage]
        at = tuple(slice(None) if d in order[:stage] else me[d] for d in "abxc")
        made = []
        for k in range(1, n[axis]):
            peer = dict(me)
            peer[axis] = lax.rem(me[axis] + k, n[axis])
            made.append(pltpu.make_async_remote_copy(
                src_ref=buf.at[at], dst_ref=buf.at[at],
                send_sem=tok_send.at[stream, stage, k], recv_sem=tok_recv.at[stream, stage, k],
                device_id=device(peer), device_id_type=MESH,
            ))
        return made

    for stage in range(4):
        for stream in range(2):
            if stage:
                for copy in gather_copies(stream, stage - 1):
                    copy.wait_recv()
            for copy in gather_copies(stream, stage):
                copy.start()
    for stream in range(2):
        for copy in gather_copies(stream, 3):
            copy.wait_recv()

    size = n_dp * PARTS * tok
    to = lax.broadcasted_iota(jnp.int32, (size, size), 0)
    came = lax.broadcasted_iota(jnp.int32, (size, size), 1)
    part, block, token = to // group, lax.rem(to, group) // tok, lax.rem(to, tok)
    perm = (came == (block * PARTS + part) * tok + token).astype(F32).astype(BF16)

    @pl.loop(0, n_e)
    def _(e):
        a, b = e // n["b"], lax.rem(e, n["b"])
        first = jnp.dot(perm, g0[a, b].reshape(size, half + LANES), preferred_element_type=F32)
        second = jnp.dot(perm, g1[a, b].reshape(size, half), preferred_element_type=F32)
        at = pl.ds(pl.multiple_of(e * group, group), group)
        for q in range(PARTS):
            mine = slice(q * group, (q + 1) * group)
            rows[q, at, 0:half] = first[mine, :half].astype(BF16)
            rows[q, at, half:slab] = second[mine].astype(BF16)
        s = [first[q * group : (q + 1) * group, half:] for q in range(3)]
        score[at, :] = s[0] + s[1] + s[2]

    tile = min(count, 128)

    def tiles(body):
        if count == tile:
            body(pl.ds(0, tile))
        else:
            @pl.loop(0, count // tile)
            def _(m):
                body(pl.ds(pl.multiple_of(m * tile, tile), tile))

    other = dict(me)
    other["c"] = lax.rem(me["c"] + 1, n["c"])

    def h_copy(e, block, peer, k):
        return pltpu.make_async_remote_copy(
            src_ref=hidden.at[e, block], dst_ref=hidden.at[e, block],
            send_sem=h_send.at[e, k], recv_sem=h_recv.at[e, k],
            device_id=device(peer), device_id_type=MESH,
        )

    def h_along_x(e):
        made = []
        for k in range(1, n["x"]):
            peer = dict(me)
            peer["x"] = lax.rem(me["x"] + k, n["x"])
            made.append(h_copy(e, dp, peer, k))
        return made

    def h_across(e, k):
        x = lax.rem(me["x"] + n["x"] - k, n["x"])
        return h_copy(e, x * n["c"] + me["c"], other, n["x"] + k)

    def forward(e):
        for k, copy in enumerate(h_along_x(e), 1):
            copy.wait_recv()
            h_across(e, k).start()

    @pl.loop(0, local)
    def _(e):
        @pl.loop(0, PARTS)
        def _(q):
            i = e * PARTS + q
            slot = lax.rem(i, ring)
            for copy in w_copies(i):
                copy.wait()

            def multiply(at):
                for j in range(2):
                    part = jnp.dot(rows[q, at, :], weights[slot, j], preferred_element_type=F32)
                    acc[j, at, :] = jnp.where(q == 0, 0.0, acc[j, at, :]) + part

            tiles(multiply)

            @pl.when(i + ring < steps)
            def _():
                for copy in w_copies(i + ring):
                    copy.start()

            @pl.when(jnp.logical_and(i + ring >= steps, i + ring - steps < down_ring))
            def _():
                d_copy(i + ring - steps).start()

        def activate(at):
            gate, up = acc[0, at, :], acc[1, at, :]
            mask = lax.broadcasted_iota(jnp.int32, (tile, LANES), 1) == ex * local + e
            weight = jnp.sum(jnp.where(mask, score[at, :], 0.0), axis=1, keepdims=True)
            hidden[e, dp, at, :] = (gate / (1.0 + jnp.exp(-gate)) * up * weight).astype(BF16)

        tiles(activate)
        for copy in h_along_x(e):
            copy.start()
        h_across(e, 0).start()

        @pl.when(e > 0)
        def _():
            forward(e - 1)

    forward(local - 1)

    def r_copy(c, k):
        return pltpu.make_async_remote_copy(
            src_ref=sent.at[c, lax.rem(ex + k, n_e)], dst_ref=arrived.at[c, k - 1],
            send_sem=r_send.at[c], recv_sem=r_recv.at[c],
            device_id=(dp, lax.rem(ex + k, n_e)), device_id_type=MESH,
        )

    @pl.loop(0, CHUNKS)
    def _(c):
        slot = lax.rem(c, down_ring)
        d_copy(c).wait()

        @pl.loop(0, local)
        def _(e):
            @pl.when(c == 0)
            def _():
                for k in range(n["x"]):
                    h_across(e, k).wait_recv()

            def multiply(at):
                part = jnp.where(e == 0, 0.0, total[at, :])
                for p in range(n_dp):
                    part += jnp.dot(
                        hidden[e, p, at, :], down[slot, e, p * ff : (p + 1) * ff, :],
                        preferred_element_type=F32,
                    )
                total[at, :] = part

            tiles(multiply)

        @pl.when(c + down_ring < CHUNKS)
        def _():
            d_copy(c + down_ring).start()

        @pl.loop(0, n_e)
        def _(k):
            sent[c, k] = total[pl.ds(pl.multiple_of(k * group, group), group), :].astype(BF16)

        @pl.loop(1, n_e)
        def _(k):
            r_copy(c, k).start()

    def f_copy(k):
        to = lax.rem(dp + k, n_dp)
        return pltpu.make_async_remote_copy(
            src_ref=fin.at[to], dst_ref=fin_in.at[k],
            send_sem=f_send.at[k], recv_sem=f_recv.at[k],
            device_id=(to, ex), device_id_type=MESH,
        )

    for c in range(CHUNKS):
        pltpu.make_async_copy(arrived.at[c], arrived.at[c], r_recv.at[c]).wait()
        value = sent[c, ex].astype(F32)
        for k in range(n_e - 1):
            value += arrived[c, k].astype(F32)
        for p in range(n_dp):
            fin[p, :, c * chunk : (c + 1) * chunk] = value[p * tok : (p + 1) * tok]
    for k in range(1, n_dp):
        f_copy(k).start()
    span = w_down.shape[2]
    for k in range(n_dp):
        came_from = lax.rem(dp + n_dp - k, n_dp)
        if k:
            f_copy(k).wait_recv()
        value = fin_in[k] if k else fin[dp]
        out[:, pl.ds(pl.multiple_of(came_from * span, LANES), span)] = value.astype(BF16)

    for stage in range(4):
        for stream in range(2):
            for copy in gather_copies(stream, stage):
                copy.wait_send()

    @pl.loop(0, local)
    def _(e):
        for copy in h_along_x(e):
            copy.wait_send()
        for k in range(n["x"]):
            h_across(e, k).wait_send()

    @pl.loop(0, CHUNKS)
    def _(c):
        pltpu.make_async_copy(arrived.at[c], arrived.at[c], r_send.at[c]).wait()

    for k in range(1, n_dp):
        f_copy(k).wait_send()


def body(tokens, routes, gate_scores, w_gate, w_up, w_down):
    n_dp, n_e = lax.axis_size("dp"), lax.axis_size("expert")
    sizes = (4, n_e // 4, n_dp // 2, 2)
    tok, width = tokens.shape
    local, _, ff = w_gate.shape
    slab, half = width // PARTS, width // PARTS // 2
    group = n_dp * tok
    count = n_e * group
    depth, span = w_down.shape[1:]
    chunk = span // CHUNKS
    ring = min(9, local * PARTS)
    down_ring = 4
    ring = max(ring, down_ring)
    sem = pltpu.SemaphoreType.DMA
    vmem = pl.BlockSpec(memory_space=pltpu.VMEM)
    hbm = pl.BlockSpec(memory_space=pl.ANY)
    return pl.pallas_call(
        functools.partial(kernel, sizes, ring, down_ring),
        out_shape=jax.ShapeDtypeStruct((tok, width), BF16),
        in_specs=[vmem] * 3 + [hbm] * 3,
        out_specs=vmem,
        scratch_shapes=[
            pltpu.VMEM(sizes + (PARTS * tok, half + LANES), BF16),
            pltpu.VMEM(sizes + (PARTS * tok, half), BF16),
            pltpu.VMEM((PARTS, count, slab), BF16),
            pltpu.VMEM((count, LANES), F32),
            pltpu.VMEM((ring, 2, slab, ff), BF16),
            pltpu.VMEM((2, count, ff), F32),
            pltpu.VMEM((local, n_dp, count, ff), BF16),
            pltpu.VMEM((down_ring, local, depth, chunk), BF16),
            pltpu.VMEM((count, chunk), F32),
            pltpu.VMEM((CHUNKS, n_e, group, chunk), BF16),
            pltpu.VMEM((CHUNKS, n_e - 1, group, chunk), BF16),
            pltpu.VMEM((n_dp, tok, span), F32),
            pltpu.VMEM((n_dp, tok, span), F32),
            sem((2, 4, max(sizes))), sem((2, 4, max(sizes))),
            sem((ring, 2)), sem((down_ring,)),
            sem((local, 2 * sizes[2])), sem((local, 2 * sizes[2])),
            sem((CHUNKS,)), sem((CHUNKS,)),
            sem((n_dp,)), sem((n_dp,)),
        ],
        compiler_params=pltpu.CompilerParams(
            collective_id=0, has_side_effects=True, vmem_limit_bytes=62 * 2**20
        ),
    )(tokens, routes, gate_scores, w_gate, w_up, w_down)


def solution(mesh):
    placed = (
        P(("dp", "expert"), None),
        P(("dp", "expert"), None),
        P(("dp", "expert"), None),
        P("expert", None, "dp"),
        P("expert", None, "dp"),
        P("expert", None, "dp"),
    )
    return jax.shard_map(
        body, mesh=mesh, in_specs=placed, out_specs=P(("dp", "expert"), None), check_vma=False
    )
```

time: 238 us -> 68.5 us (0.29)
  blocking collectives: 116 us -> 0 us
  Pallas kernels: 0 us -> 66.8 us
  matrix products: 42.8 us -> 0 us
  waiting for transfers between devices: 38.2 us -> 0 us
  local copies, waits for them, and re-layouts: 20.9 us -> 1.46 us
  between operations: 13.5 us -> 0.01 us
  starting transfers between devices: 5.52 us -> 0 us
    all_to_all x2 -> x0, blocking collectives: 104 us -> none  [the longest x1 88.2 us: body(): lax.all_to_all(outgoing, 'expert', split_axis=0, concat_axis=2, tiled=True)]
    pallas_call x0 -> x1, Pallas kernels: none -> 66.8 us  [body(): pl.pallas_call(functools.partial(kernel, sizes, ring, down_ring), out_sha...]
    dot_general x5 -> x0, matrix products: 42.8 us -> none  [the longest x1 14.6 us: body(): jnp.einsum('erf,efk->erk', lax.all_gather(hidden, 'dp', axis=2, tiled=Tru...]
    all_to_all x1 -> x0, waiting for transfers between devices: 22.2 us -> none  [body(): lax.all_to_all(lax.all_to_all(expert_out, 'dp', split_axis=1, concat_axis...]
    all_gather x1 -> x0, waiting for transfers between devices: 15.9 us -> none  [body(): lax.all_gather(hidden, 'dp', axis=2, tiled=True)]
    all_gather x2 -> x0, blocking collectives: 12.5 us -> none  [the longest x1 6.26 us: body(): lax.all_gather(tokens, 'dp', axis=0, tiled=True)]
    reshape x4 -> x0, local copies, waits for them, and re-layouts: 9.18 us -> none  [the longest x1 8.4 us: body(): merged = arrived.reshape(local_experts, items * arrived.shape[2], D)]
    all_to_all x3 -> x0, local copies, waits for them, and re-layouts: 7.47 us -> none  [the longest x1 5.49 us: body(): lax.all_to_all(outgoing, 'expert', split_axis=0, concat_axis=2, tiled=True)]
  transfers between devices with their start and end apart: 2 -> 0, of which waited for: 2 -> 0; matrix products, arithmetic and copies ran while one was open for 0% -> 0% of each run, Pallas kernels for 0% -> 0%
where the time goes in v1:
time: 68.5 us; the launch traced here: 68.3 us
  Pallas kernels  66.8 us (98%)
  local copies, waits for them, and re-layouts  1.46 us (2%)
    pallas_call x1, Pallas kernels, body(): pl.pallas_call(functools.partial(kernel, sizes, ring, down_ring), out_sha...  66.8 us
    unnamed x1, local copies, waits for them, and re-layouts  1.46 us

profile of v1, /device:TPU:0, one launch (start us, length us, event | category | flops | bytes accessed | tf_op | source)
XLA Modules:
  0.0 68.3 jit_solution(2865978643276732877)
XLA Ops:
  0.0 66.8 %shard_map.64 = bf16[4,7168]{1,0:T(4,128)(2,1)} custom-call(bf16[4,7168]{1,0:T(4,128)(2,1)} %tokens.1, s32[4,8]{1,0:T(4,128)} %routes.1, f32[4,8]{1,0:T(4,128)} %scores.1, bf16[4,7168,512]{2,1,0:T(8,128)(2,1)} %w_gate.1, bf16[4,7168,512]{2,1,0:T(8,128)(2,1)} %w_up.1, bf16[4,2048,1792]{2,1,0:T(8,128)(2,1)} %w_down.1), custom_call_target="tpu_custom_call" | custom-call | tf_op jit(solution)/shard_map/pallas_call | solution.py:314
  66.8 1.5 %copy.8 = bf16[4,7168]{1,0:T(4,128)(2,1)} copy(bf16[4,7168]{1,0:T(4,128)(2,1)} %shard_map.64) | data formatting | bytes 114688

commit v2 on v1

--- a/solution.py
+++ b/solution.py
@@ -13,7 +13,7 @@
 CHUNKS = 7
 LANES = 128
 
-ORDERS = (("a", "b", "x", "c"), ("x", "b", "a", "c"))
+ORDERS = (('a', 'b', 'x', 'c'), ('a', 'x', 'b', 'c'))
 
 
 def kernel(
@@ -57,6 +57,10 @@
         for copy in w_copies(i):
             copy.start()
 
+    @pl.loop(0, down_ring)
+    def _(i):
+        d_copy(i).start()
+
     barrier = pltpu.get_barrier_semaphore()
     for k in range(1, n_dp):
         pl.semaphore_signal(barrier, inc=1, device_id=(lax.rem(dp + k, n_dp), ex), device_id_type=MESH)
@@ -187,10 +191,6 @@
                 for copy in w_copies(i + ring):
                     copy.start()
 
-            @pl.when(jnp.logical_and(i + ring >= steps, i + ring - steps < down_ring))
-            def _():
-                d_copy(i + ring - steps).start()
-
         def activate(at):
             gate, up = acc[0, at, :], acc[1, at, :]
             mask = lax.broadcasted_iota(jnp.int32, (tile, LANES), 1) == ex * local + e
@@ -205,8 +205,6 @@
         @pl.when(e > 0)
         def _():
             forward(e - 1)
-
-    forward(local - 1)
 
     def r_copy(c, k):
         return pltpu.make_async_remote_copy(
@@ -215,28 +213,55 @@
             device_id=(dp, lax.rem(ex + k, n_e)), device_id_type=MESH,
         )
 
-    @pl.loop(0, CHUNKS)
+    def project(c, e, first):
+        slot = lax.rem(c, down_ring)
+
+        def multiply(at):
+            part = jnp.where(first, 0.0, total[slot, at, :])
+            for p in range(n_dp):
+                part += jnp.dot(
+                    hidden[e, p, at, :], down[slot, e, p * ff : (p + 1) * ff, :],
+                    preferred_element_type=F32,
+                )
+            total[slot, at, :] = part
+
+        tiles(multiply)
+
+    before = local - 1
+
+    @pl.loop(0, down_ring)
     def _(c):
-        slot = lax.rem(c, down_ring)
         d_copy(c).wait()
 
-        @pl.loop(0, local)
+        @pl.loop(0, before)
         def _(e):
             @pl.when(c == 0)
             def _():
                 for k in range(n["x"]):
                     h_across(e, k).wait_recv()
 
-            def multiply(at):
-                part = jnp.where(e == 0, 0.0, total[at, :])
-                for p in range(n_dp):
-                    part += jnp.dot(
-                        hidden[e, p, at, :], down[slot, e, p * ff : (p + 1) * ff, :],
-                        preferred_element_type=F32,
-                    )
-                total[at, :] = part
-
-            tiles(multiply)
+            project(c, e, e == 0)
+
+        @pl.when(c == min(1, down_ring - 1))
+        def _():
+            forward(local - 1)
+
+    for k in range(n["x"]):
+        h_across(local - 1, k).wait_recv()
+
+    @pl.loop(0, CHUNKS)
+    def _(c):
+        slot = lax.rem(c, down_ring)
+
+        @pl.when(c >= down_ring)
+        def _():
+            d_copy(c).wait()
+
+            @pl.loop(0, before)
+            def _(e):
+                project(c, e, e == 0)
+
+        project(c, before, before == 0)
 
         @pl.when(c + down_ring < CHUNKS)
         def _():
@@ -244,7 +269,7 @@
 
         @pl.loop(0, n_e)
         def _(k):
-            sent[c, k] = total[pl.ds(pl.multiple_of(k * group, group), group), :].astype(BF16)
+            sent[c, k] = total[slot, pl.ds(pl.multiple_of(k * group, group), group), :].astype(BF16)
 
         @pl.loop(1, n_e)
         def _(k):
@@ -307,7 +332,6 @@
     chunk = span // CHUNKS
     ring = min(9, local * PARTS)
     down_ring = 4
-    ring = max(ring, down_ring)
     sem = pltpu.SemaphoreType.DMA
     vmem = pl.BlockSpec(memory_space=pltpu.VMEM)
     hbm = pl.BlockSpec(memory_space=pl.ANY)
@@ -325,7 +349,7 @@
             pltpu.VMEM((2, count, ff), F32),
             pltpu.VMEM((local, n_dp, count, ff), BF16),
             pltpu.VMEM((down_ring, local, depth, chunk), BF16),
-            pltpu.VMEM((count, chunk), F32),
+            pltpu.VMEM((down_ring, count, chunk), F32),
             pltpu.VMEM((CHUNKS, n_e, group, chunk), BF16),
             pltpu.VMEM((CHUNKS, n_e - 1, group, chunk), BF16),
             pltpu.VMEM((n_dp, tok, span), F32),

time: 68.5 us -> 63.7 us (0.930)
  Pallas kernels: 66.8 us -> 62 us
    pallas_call x1, Pallas kernels: 66.8 us -> 62 us  [body(): pl.pallas_call(functools.partial(kernel, sizes, ring, down_ring), out_sha...]
where the time goes in v2:
time: 63.7 us; the launch traced here: 63.4 us
  Pallas kernels  62 us (97%)
  local copies, waits for them, and re-layouts  1.46 us (2%)
    pallas_call x1, Pallas kernels, body(): pl.pallas_call(functools.partial(kernel, sizes, ring, down_ring), out_sha...  62 us
    unnamed x1, local copies, waits for them, and re-layouts  1.46 us

profile of v2, /device:TPU:0, one launch (start us, length us, event | category | flops | bytes accessed | tf_op | source)
XLA Modules:
  0.0 63.4 jit_solution(4080120546340702504)
XLA Ops:
  0.0 62.0 %shard_map.64 = bf16[4,7168]{1,0:T(4,128)(2,1)} custom-call(bf16[4,7168]{1,0:T(4,128)(2,1)} %tokens.1, s32[4,8]{1,0:T(4,128)} %routes.1, f32[4,8]{1,0:T(4,128)} %scores.1, bf16[4,7168,512]{2,1,0:T(8,128)(2,1)} %w_gate.1, bf16[4,7168,512]{2,1,0:T(8,128)(2,1)} %w_up.1, bf16[4,2048,1792]{2,1,0:T(8,128)(2,1)} %w_down.1), custom_call_target="tpu_custom_call" | custom-call | tf_op jit(solution)/shard_map/pallas_call | solution.py:338
  62.0 1.5 %copy.8 = bf16[4,7168]{1,0:T(4,128)(2,1)} copy(bf16[4,7168]{1,0:T(4,128)(2,1)} %shard_map.64) | data formatting | bytes 114688
